TPU v7x, 32 devices: a whole 2x2x4 slice. The times are simulated.
32 devices in a mesh: grp: 2 (over x), row: 4 (over y, core), col: 4 (over z).
Axes of the slice: x: 2, y: 2, z: 4, core: 2. Of those that a mesh axis runs over, the one named last changes fastest.
Arguments:
- amplitudes: bfloat16 [64, 4, 256, 256], P(('grp', 'row'), 'col'), may hold values from -6 to 6
- factors: bfloat16 [4, 256, 256], P('col'), may hold values from -0.1875 to 0.1875
- cycle_weight: bfloat16 [16384, 16384], P('col', 'row'), may hold values from -0.046875 to 0.046875
- orbital_order: int32 [256], replicated, may hold values from 0 to 255, each once
Outputs:
- ladder_term: bfloat16 [64, 4, 256, 256], P(('grp', 'row'), 'col')
- cycle_term: bfloat16 [1024, 16384], P(('grp', 'row'), 'col')
Inputs may be any that keep to these rules, and one draw needn't show every extreme that they name: `orbital_order`: each of 0 to 255 appears exactly once.
All inputs are finite; a program needn't handle non-finite values.
Results may differ from a plain program's by a relative error of at most 0.0049.
Values may be sent and summed in bfloat16 or wider, within the bound.
A program may use at most 128 MiB of HBM per device.

v0:
```python
import jax
import jax.numpy as jnp
from jax import lax
from jax.sharding import PartitionSpec as P


def dress_pairs(factor_piece, pair_stack):
    dressed = jnp.einsum(
        "pac,qcd->pqad", factor_piece, pair_stack, preferred_element_type=jnp.float32
    ).astype(jnp.bfloat16)
    return jnp.einsum("pqad,pbd->qab", dressed, factor_piece, preferred_element_type=jnp.float32)


def shards(amplitudes, factors, cycle_weight, orbital_order):
    occ_rows = amplitudes.shape[0]
    occ_cols = amplitudes.shape[1]
    virtual = amplitudes.shape[2]
    pair_stack = amplitudes.reshape(occ_rows * occ_cols, virtual, virtual)
    ladder_sum = dress_pairs(lax.all_gather(factors, "col", axis=0, tiled=True), pair_stack)
    ladder_sum = ladder_sum.reshape(occ_rows, occ_cols, virtual, virtual)
    ladder_term = ladder_sum.astype(jnp.bfloat16)
    groups = lax.axis_size("grp")
    row_count = lax.axis_size("row")
    panel_width = virtual // groups
    block_width = virtual // row_count
    ordered = jnp.take(amplitudes, orbital_order, axis=3)
    ordered = ordered.reshape(occ_rows, occ_cols, row_count, block_width, groups, panel_width)
    outgoing = jnp.transpose(ordered, (4, 2, 3, 0, 1, 5))
    outgoing = outgoing.reshape(groups * row_count, block_width, 1, occ_rows, occ_cols, panel_width)
    arrived = lax.all_to_all(outgoing, ("grp", "row"), split_axis=0, concat_axis=2, tiled=True)
    column_tile = arrived.reshape(
        block_width * groups * row_count * occ_rows, occ_cols * panel_width
    )
    products = lax.dot_general(
        lax.all_gather(column_tile, "col", axis=1, tiled=True),
        cycle_weight,
        (((0,), (1,)), ((), ())),
        preferred_element_type=jnp.float32,
    )
    cycle_term = lax.psum_scatter(products, "row", scatter_dimension=0, tiled=True).astype(
        jnp.bfloat16
    )
    return (ladder_term, cycle_term)


def solution(mesh):
    return jax.shard_map(
        shards,
        mesh=mesh,
        in_specs=(P(("grp", "row"), "col", None, None), P("col", None, None), P("col", "row"), P()),
        out_specs=(P(("grp", "row"), "col", None, None), P(("grp", "row"), "col")),
        check_vma=False,
    )
```

profile of v0, /device:TPU:24, one launch (start us, length us, event | category | flops | bytes accessed | tf_op | source)
XLA Modules:
  0.0 217.8 jit_solution(12071950283012990343)
XLA Ops:
  7.2 0.0 all-gather.2.cloned.1.call-start
  7.2 0.7 compare_select_fusion
  7.9 0.7 and_bitcast_fusion
  8.6 1.9 copy.18
  10.5 0.8 gather_fusion
  11.2 0.8 copy.21
  12.0 0.3 gather.7
  12.3 0.9 fusion.10
  13.2 0.7 copy.22
  13.9 18.1 %all_to_all.15 = bf16[8,64,1,8,1,128]{5,3,1,4,2,0:T(8,128)(2,1)S(1)} all-to-all(bf16[8,64,1,8,1,128]{5,3,1,4,2,0:T(8,128)(2,1)S(1)} %bitcast.44), channel_id=1, replica_groups=mesh['grp'=2,'row'=4,'col'=4] {'grp','row'}, dimensions={0} | all-to-all | bytes 2097152 | tf_op jit(solution)/shard_map/all_to_all | solution.py:30
  32.0 1.3 copy.24
  33.3 0.0 all-gather.2.cloned.1.call-update
  33.3 0.0 reduce-scatter.2.cloned.1.call-start
  33.4 77.8 %all-gather.2.cloned.1.call-done = bf16[4096,512]{1,0:T(8,128)(2,1)} async-done(((bf16[4096,128]{1,0:T(8,128)(2,1)}), bf16[4096,512]{1,0:T(8,128)(2,1)}) %all-gather.2.cloned.1.call-update) | async-done | bytes 4194320 | tf_op jit(solution)/shard_map/all_gather | solution.py:35
  111.2 24.1 %fusion.15 = f32[512,4096]{1,0:T(8,128)} fusion(bf16[4096,512]{1,0:T(8,128)(2,1)} %all-gather.2.cloned.1.call-done, bf16[4096,4096]{1,0:T(8,128)(2,1)} %param.6), kind=kOutput, calls=%fused_computation.14 | convolution fusion | flops 17179869184 | bytes 46137344 | tf_op jit(solution)/shard_map/dot_general | solution.py:34
  135.4 0.0 copy-start.1
  135.4 0.0 copy-start
  135.4 0.0 reduce-scatter.2.cloned.1.call-update
  135.4 0.9 copy-done.1
  136.3 15.7 %all_gather.6 = bf16[4,256,256]{2,1,0:T(8,128)(2,1)S(1)} all-gather(bf16[1,256,256]{2,1,0:T(8,128)(2,1)S(1)} %copy-done.1), channel_id=1, replica_groups=mesh['grp'=2,'row'=4,'col'=4] {'col'}, dimensions={0}, use_global_device_ids=true | all-gather | bytes 655360 | tf_op jit(solution)/shard_map/all_gather | solution.py:19
  152.0 0.0 copy-done
  152.0 4.1 %fusion.7 = bf16[8,1,256,256]{3,2,1,0:T(8,128)(2,1)} fusion(bf16[8,1,256,256]{3,2,1,0:T(8,128)(2,1)S(1)} %copy-done, bf16[4,256,256]{2,1,0:T(8,128)(2,1)S(1)} %all_gather.6), kind=kOutput, calls=%fused_computation.7 | convolution fusion | flops 2150105088 | bytes 2621440 | tf_op jit(solution)/shard_map/pqad,pbd->qab/dot_general | solution.py:11
  156.1 52.2 %reduce-scatter.2.cloned.1.call-done = f32[128,4096]{1,0:T(8,128)} async-done(((f32[512,4096]{1,0:T(8,128)}), f32[128,4096]{1,0:T(8,128)}) %reduce-scatter.2.cloned.1.call-update) | async-done | bytes 2097168 | tf_op jit(solution)/shard_map/reduce_scatter | solution.py:40
  208.3 2.7 %convert_element_type.19 = bf16[128,4096]{1,0:T(8,128)(2,1)} convert(f32[128,4096]{1,0:T(8,128)} %reduce-scatter.2.cloned.1.call-done) | non-fusion elementwise | flops 524288 | bytes 3145728 | tf_op jit(solution)/shard_map/convert_element_type | solution.py:40
  (1 shorter events, 0.0 us)
Async XLA Ops:
  7.2 104.1 %all-gather.2.cloned.1.call-start = ((), (), s32[]{:S(2)}) async-start(), calls=%async_computation.2 | async-start | bytes 5242880 | tf_op jit(solution)/shard_map/all_gather | solution.py:35
  33.3 175.0 %reduce-scatter.2.cloned.1.call-start = ((), (), s32[]{:S(2)}) async-start(), calls=%async_computation.3 | async-start | bytes 10485760 | tf_op jit(solution)/shard_map/reduce_scatter | solution.py:40
  135.4 0.9 copy-start.1
  135.4 16.6 %copy-start = (bf16[8,1,256,256]{3,2,1,0:T(8,128)(2,1)S(1)}, bf16[8,1,256,256]{3,2,1,0:T(8,128)(2,1)}, u32[]{:S(2)}) copy-start(bf16[8,1,256,256]{3,2,1,0:T(8,128)(2,1)} %param.4) | copy-start | bytes 3145732
Sparse Core Ops, SparseCore 0:
  33.4 77.7 all-gather.1
  135.5 72.7 reduce-scatter.1
where the time goes:
time: 220 us; the launch traced here: 218 us
  waiting for transfers between devices  130 us (59%)
  blocking collectives  33.8 us (15%)
  matrix products  28.2 us (13%)
  between operations  14.1 us (6%)
  local copies, waits for them, and re-layouts  6.52 us (3%)
  other arithmetic  4.97 us (2%)
    all_gather x1, waiting for transfers between devices, shards(): lax.all_gather(column_tile, 'col', axis=1, tiled=True)  77.8 us
    reduce_scatter x1, waiting for transfers between devices, shards(): lax.psum_scatter(products, 'row', scatter_dimension=0, tiled=True)  52.2 us
    dot_general x1, matrix products, shards(): lax.dot_general(lax.all_gather(column_tile, 'col', axis=1, tiled=True), c...  24.1 us
    all_to_all x1, blocking collectives, shards(): lax.all_to_all(outgoing, ('grp', 'row'), split_axis=0, concat_axis=2, til...  18.1 us
    all_gather x1, blocking collectives, shards(): lax.all_gather(factors, 'col', axis=0, tiled=True)  15.7 us
  transfers between devices with their start and end apart: 2, of which 2 were waited for; matrix products, arithmetic and copies ran while one was open for 2% of the time, Pallas kernels for 0%

commit v1 on v0

--- a/solution.py
+++ b/solution.py
@@ -1,7 +1,17 @@
+import functools
+
 import jax
 import jax.numpy as jnp
 from jax import lax
+from jax.experimental import pallas as pl
+from jax.experimental.pallas import tpu as pltpu
 from jax.sharding import PartitionSpec as P
+
+MESH = pl.DeviceIdType.MESH
+TILE = 16
+LANES = 128
+PARTS = 4
+NT = (((1,), (1,)), ((), ()))
 
 
 def dress_pairs(factor_piece, pair_stack):
@@ -11,7 +21,7 @@
     return jnp.einsum("pqad,pbd->qab", dressed, factor_piece, preferred_element_type=jnp.float32)
 
 
-def shards(amplitudes, factors, cycle_weight, orbital_order):
+def plain_shards(amplitudes, factors, cycle_weight, orbital_order):
     occ_rows = amplitudes.shape[0]
     occ_cols = amplitudes.shape[1]
     virtual = amplitudes.shape[2]
@@ -43,6 +53,444 @@
     return (ladder_term, cycle_term)
 
 
+def kernel(
+    sizes, order_ref, amp, fac, weight, ladder_out, cycle_out,
+    wv, own, other, staged, panel, acc, pair_out, pair_in, far_out, far_in, result, fitted,
+    load_sem, weight_sem, raw_send, raw_recv, ex_send, ex_recv, up_send, down_send, z_recv,
+    fit_send, fit_recv, fan_send, fan_recv, pair_send, pair_recv, far_send, far_recv, out_sem,
+):
+    groups, rows, cols = sizes
+    sides = rows // 2
+    chips = groups * sides
+    pairs, virtual, _ = amp.shape
+    block = virtual // rows
+    chunks = block // TILE
+    depth = weight.shape[1] // chunks
+    span = weight.shape[0] // PARTS
+    panel_width = virtual // groups
+    g, r, z = lax.axis_index("grp"), lax.axis_index("row"), lax.axis_index("col")
+    side, core = r // 2, r % 2
+    mate = side * 2 + 1 - core
+    chip = g * sides + side
+    place = g * rows + r
+    fit_rows = virtual // (groups * rows)
+
+    def at(gg, rr, zz):
+        return {"grp": gg, "row": rr, "col": zz}
+
+    def remote(src, dst, send, recv, where):
+        return pltpu.make_async_remote_copy(
+            src_ref=src, dst_ref=dst, send_sem=send, recv_sem=recv,
+            device_id=where, device_id_type=MESH,
+        )
+
+    mine = pl.ds(pl.multiple_of(place * fit_rows, fit_rows), fit_rows)
+    load_own = pltpu.make_async_copy(amp, own, load_sem.at[0])
+    load_own.start()
+    load_fit = pltpu.make_async_copy(fac.at[0, mine], fitted.at[z, mine], load_sem.at[1])
+    load_fit.start()
+
+    def load_weight(c):
+        return pltpu.make_async_copy(
+            weight.at[:, pl.ds(c * depth, depth)], wv.at[c], weight_sem.at[c]
+        )
+
+    for c in range(chunks):
+        load_weight(c).start()
+
+    peers = groups * rows - 1
+    barrier = pltpu.get_barrier_semaphore()
+    for step in range(1, peers + 1):
+        q = lax.rem(place + step, groups * rows)
+        pl.semaphore_signal(barrier, inc=1, device_id=at(q // rows, q % rows, z), device_id_type=MESH)
+    for step in range(1, cols):
+        pl.semaphore_signal(
+            barrier, inc=1, device_id=at(g, r, lax.rem(z + step, cols)), device_id_type=MESH
+        )
+    pl.semaphore_wait(barrier, peers + cols - 1)
+
+    def raw_copy(s):
+        first = pl.multiple_of((s * 2 + 1 - core) * block, block)
+        return remote(
+            amp.at[:, pl.ds(first, block)], other.at[s], raw_send.at[s], raw_recv.at[s],
+            at(g, mate, z),
+        )
+
+    for s in range(sides):
+        raw_copy(s).start()
+
+    load_fit.wait()
+
+    def fit_copy(step):
+        here = fitted.at[z, mine]
+        return remote(
+            here, here, fit_send.at[step - 1], fit_recv.at[step - 1],
+            at(g, r, lax.rem(z + step, cols)),
+        )
+
+    for step in range(1, cols):
+        fit_copy(step).start()
+
+    load_own.wait()
+
+    width = 2 * pairs * TILE
+    pick = (
+        lax.broadcasted_iota(jnp.int32, (virtual, virtual), 0) == order_ref[...]
+    ).astype(jnp.float32).astype(jnp.bfloat16)
+    to_row = lax.broadcasted_iota(jnp.int32, (width, width), 0)
+    from_row = lax.broadcasted_iota(jnp.int32, (width, width), 1)
+    k_row = to_row & (2 * pairs - 1)
+    c_row = to_row // (2 * pairs)
+    late = (k_row // pairs) ^ core
+    turn = (
+        from_row == late * (pairs * TILE) + (k_row & (pairs - 1)) * TILE + c_row
+    ).astype(jnp.float32).astype(jnp.bfloat16)
+
+    slot = pl.ds(pl.multiple_of(chip * TILE, TILE), TILE)
+
+    def ex_copy(c, s, q):
+        return remote(
+            staged.at[c, s, q], panel.at[z, c, :, slot, :],
+            ex_send.at[c, s * groups + q], ex_recv.at[c, chip], at(q, s * 2 + core, z),
+        )
+
+    for s in range(sides):
+        raw_copy(s).wait_recv()
+
+    def exchange(c, carry):
+        for s in range(sides):
+            first = pl.multiple_of((s * 2 + core) * block + c * TILE, TILE)
+            near = own[:, pl.ds(first, TILE), :].reshape(pairs * TILE, virtual)
+            far = other[s, :, pl.ds(pl.multiple_of(c * TILE, TILE), TILE), :].reshape(
+                pairs * TILE, virtual
+            )
+            both = jnp.concatenate([near, far], axis=0)
+            picked = jnp.dot(both, pick, preferred_element_type=jnp.float32).astype(jnp.bfloat16)
+            turned = jnp.dot(turn, picked, preferred_element_type=jnp.float32).astype(jnp.bfloat16)
+            for q in range(groups):
+                part = turned[:, q * panel_width:(q + 1) * panel_width]
+                part = part.reshape(TILE, 2 * pairs, panel_width)
+                here = (q == g) & (s == side)
+
+                @pl.when(here)
+                def _():
+                    panel[z, c, :, slot, :] = part
+
+                @pl.when(jnp.logical_not(here))
+                def _():
+                    staged[c, s, q] = part
+                    ex_copy(c, s, q).start()
+        return carry
+
+    lax.fori_loop(0, chunks, exchange, 0)
+
+    def up_copy(j, c):
+        piece = panel.at[j, c]
+        return remote(piece, piece, up_send.at[j, c], z_recv.at[j, c], at(g, r, z + 1))
+
+    def down_copy(j, c):
+        piece = panel.at[j, c]
+        return remote(piece, piece, down_send.at[j, c], z_recv.at[j, c], at(g, r, z - 1))
+
+    def multiply(j, c, first):
+        piece = panel[j, c].reshape(depth, panel_width)
+
+        def one(i, carry):
+            sl = pl.ds(pl.multiple_of(i * span, span), span)
+            product = jnp.dot(wv[c, sl, :], piece, preferred_element_type=jnp.float32)
+            if first:
+                @pl.when(c == 0)
+                def _():
+                    acc[j, sl, :] = product
+
+                @pl.when(c > 0)
+                def _():
+                    acc[j, sl, :] += product
+            else:
+                acc[j, sl, :] = jnp.where(c == 0, product, acc[j, sl, :] + product)
+            return carry
+
+        lax.fori_loop(0, PARTS, one, 0)
+
+    def pair_copy(j, i):
+        sl = pl.ds(pl.multiple_of(i * span, span), span)
+        h = j // 2
+        return remote(
+            pair_out.at[h, sl], pair_in.at[h, sl], pair_send.at[h, i], pair_recv.at[h, i],
+            at(g, mate, z),
+        )
+
+    def far_copy(i):
+        sl = pl.ds(pl.multiple_of(i * span, span), span)
+        return remote(
+            far_out.at[sl], far_in.at[sl], far_send.at[i], far_recv.at[i],
+            at(g, (1 - side) * 2 + core, z),
+        )
+
+    def give(j):
+        @pl.when(j % 2 != core)
+        def _():
+            def one(i, carry):
+                sl = pl.ds(pl.multiple_of(i * span, span), span)
+                pair_out[j // 2, sl, :] = acc[j, sl, :].astype(jnp.bfloat16)
+                pair_copy(j, i).start()
+                return carry
+
+            lax.fori_loop(0, PARTS, one, 0)
+
+    def pass_on(j):
+        @pl.when((j % 2 == core) & (j // 2 != side))
+        def _():
+            def one(i, carry):
+                sl = pl.ds(pl.multiple_of(i * span, span), span)
+                pair_copy(j, i).wait_recv()
+                total = acc[j, sl, :] + pair_in[j // 2, sl, :].astype(jnp.float32)
+                far_out[sl, :] = total.astype(jnp.bfloat16)
+                far_copy(i).start()
+                return carry
+
+            lax.fori_loop(0, PARTS, one, 0)
+
+    def first_hop(c, carry):
+        for q in range(chips):
+            @pl.when(q != chip)
+            def _():
+                landing = panel.at[z, c, :, pl.ds(q * TILE, TILE), :]
+                remote(
+                    landing, landing, ex_send.at[c, 0], ex_recv.at[c, q], at(g, mate, z)
+                ).wait_recv()
+
+        @pl.when(z + 1 < cols)
+        def _():
+            up_copy(z, c).start()
+
+        @pl.when(z > 0)
+        def _():
+            down_copy(z, c).start()
+
+        load_weight(c).wait()
+        multiply(z, c, True)
+        return carry
+
+    lax.fori_loop(0, chunks, first_hop, 0)
+
+    def fan_copy(step):
+        q = lax.rem(place + step, groups * rows)
+        here = fitted.at[:, mine]
+        return remote(
+            here, here, fan_send.at[step - 1], fan_recv.at[step - 1], at(q // rows, q % rows, z)
+        )
+
+    for step in range(1, cols):
+        fit_copy(step).wait_recv()
+    for step in range(1, peers + 1):
+        fan_copy(step).start()
+    give(z)
+    pass_on(z)
+
+    def ladder(k):
+        left = own[k]
+        total = jnp.zeros((virtual, virtual), jnp.float32)
+        for p in range(cols):
+            dressed = jnp.dot(fitted[p], left, preferred_element_type=jnp.float32)
+            total += lax.dot_general(
+                dressed.astype(jnp.bfloat16), fitted[p], NT, preferred_element_type=jnp.float32
+            )
+        own[k] = total.astype(jnp.bfloat16)
+
+    def hop(n, carry):
+        low, high = z - n, z + n
+
+        def step(c, inner):
+            @pl.when(low >= 0)
+            def _():
+                up_copy(low, c).wait_recv()
+
+                @pl.when(z + 1 < cols)
+                def _():
+                    up_copy(low, c).start()
+
+            @pl.when(high < cols)
+            def _():
+                down_copy(high, c).wait_recv()
+
+                @pl.when(z > 0)
+                def _():
+                    down_copy(high, c).start()
+
+            @pl.when(low >= 0)
+            def _():
+                multiply(low, c, True)
+
+            @pl.when(high < cols)
+            def _():
+                multiply(high, c, True)
+
+            return inner
+
+        lax.fori_loop(0, chunks, step, 0)
+        for j, valid in ((low, low >= 0), (high, high < cols)):
+            @pl.when(valid)
+            def _():
+                give(j)
+        for j, valid in ((low, low >= 0), (high, high < cols)):
+            @pl.when(valid)
+            def _():
+                pass_on(j)
+
+        @pl.when(n == 1)
+        def _():
+            for step in range(1, peers + 1):
+                fan_copy(step).wait_recv()
+
+            def one(k, inner):
+                ladder(k)
+                return inner
+
+            lax.fori_loop(0, pairs, one, 0)
+            pltpu.make_async_copy(own, ladder_out, load_sem.at[0]).start()
+
+        return carry
+
+    lax.fori_loop(1, cols, hop, 0)
+
+    def out_copy(i):
+        return pltpu.make_async_copy(
+            result.at[i], cycle_out.at[:, pl.ds(i * span, span)], out_sem.at[i]
+        )
+
+    for i in range(PARTS):
+        sl = pl.ds(i * span, span)
+        pair_copy(r, i).wait_recv()
+        far_copy(i).wait_recv()
+        total = acc[r, sl, :] + pair_in[side, sl, :].astype(jnp.float32)
+        total += far_in[sl, :].astype(jnp.float32)
+        result[i] = total.T.astype(jnp.bfloat16)
+        out_copy(i).start()
+
+    pltpu.make_async_copy(own, ladder_out, load_sem.at[0]).wait()
+    for s in range(sides):
+        raw_copy(s).wait_send()
+    for step in range(1, cols):
+        fit_copy(step).wait_send()
+    for step in range(1, peers + 1):
+        fan_copy(step).wait_send()
+
+    def drain(c, carry):
+        for s in range(sides):
+            for q in range(groups):
+                @pl.when(jnp.logical_not((q == g) & (s == side)))
+                def _():
+                    ex_copy(c, s, q).wait_send()
+        for j in range(cols):
+            @pl.when((j <= z) & (z + 1 < cols))
+            def _():
+                up_copy(j, c).wait_send()
+
+            @pl.when((j >= z) & (z > 0))
+            def _():
+                down_copy(j, c).wait_send()
+        return carry
+
+    lax.fori_loop(0, chunks, drain, 0)
+    for i in range(PARTS):
+        for h in range(sides):
+            pair_copy(2 * h, i).wait_send()
+        far_copy(i).wait_send()
+        out_copy(i).wait()
+
+
+def fused_shards(sizes, amplitudes, factors, cycle_weight, orbital_order):
+    groups, rows, cols = sizes
+    pairs, one, virtual, _ = amplitudes.shape
+    out_width, depth = cycle_weight.shape
+    block = virtual // rows
+    chunks = block // TILE
+    chips = groups * rows // 2
+    panel_width = virtual // groups
+    span = out_width // PARTS
+    half = jnp.bfloat16
+    dma = pltpu.SemaphoreType.DMA
+    anywhere = pl.BlockSpec(memory_space=pl.ANY)
+    matmuls = 2 * out_width * depth * cols * panel_width
+    ladder_term, cycle_term = pl.pallas_call(
+        functools.partial(kernel, sizes),
+        out_shape=(
+            jax.ShapeDtypeStruct((pairs, virtual, virtual), half),
+            jax.ShapeDtypeStruct((panel_width, out_width), half),
+        ),
+        in_specs=[pl.BlockSpec(memory_space=pltpu.VMEM), anywhere, anywhere, anywhere],
+        out_specs=(anywhere, anywhere),
+        scratch_shapes=[
+            pltpu.VMEM((chunks, out_width, depth // chunks), half),
+            pltpu.VMEM((pairs, virtual, virtual), half),
+            pltpu.VMEM((rows // 2, pairs, block, virtual), half),
+            pltpu.VMEM((chunks, rows // 2, groups, TILE, 2 * pairs, panel_width), half),
+            pltpu.VMEM((cols, chunks, TILE, 2 * pairs * chips, panel_width), half),
+            pltpu.VMEM((cols, out_width, panel_width), jnp.float32),
+            pltpu.VMEM((rows // 2, out_width, panel_width), half),
+            pltpu.VMEM((rows // 2, out_width, panel_width), half),
+            pltpu.VMEM((out_width, panel_width), half),
+            pltpu.VMEM((out_width, panel_width), half),
+            pltpu.VMEM((PARTS, panel_width, span), half),
+            pltpu.VMEM((cols, virtual, virtual), half),
+            dma((2,)),
+            dma((chunks,)),
+            dma((rows // 2,)),
+            dma((rows // 2,)),
+            dma((chunks, chips)),
+            dma((chunks, chips)),
+            dma((cols, chunks)),
+            dma((cols, chunks)),
+            dma((cols, chunks)),
+            dma((cols - 1,)),
+            dma((cols - 1,)),
+            dma((groups * rows - 1,)),
+            dma((groups * rows - 1,)),
+            dma((rows // 2, PARTS)),
+            dma((rows // 2, PARTS)),
+            dma((PARTS,)),
+            dma((PARTS,)),
+            dma((PARTS,)),
+        ],
+        compiler_params=pltpu.CompilerParams(
+            collective_id=0, has_side_effects=True, vmem_limit_bytes=60 * 1024 * 1024
+        ),
+        cost_estimate=pl.CostEstimate(
+            flops=matmuls, bytes_accessed=2 * out_width * depth, transcendentals=0
+        ),
+    )(
+        orbital_order.reshape(1, virtual),
+        amplitudes.reshape(pairs, virtual, virtual),
+        factors,
+        cycle_weight,
+    )
+    return ladder_term.reshape(pairs, one, virtual, virtual), cycle_term
+
+
+def shards(amplitudes, factors, cycle_weight, orbital_order):
+    groups, rows, cols = (lax.axis_size(name) for name in ("grp", "row", "col"))
+    pairs, per_col, virtual, _ = amplitudes.shape
+    out_width, depth = cycle_weight.shape
+    fits = (
+        per_col == 1
+        and factors.shape[0] == 1
+        and rows == cols
+        and rows // 2 == 2
+        and rows % 2 == 0
+        and 2 * pairs == TILE
+        and virtual == groups * LANES
+        and virtual % (rows * TILE) == 0
+        and virtual % (groups * rows * TILE) == 0
+        and depth == virtual // rows * groups * rows * pairs
+        and out_width % (PARTS * LANES) == 0
+        and 2 * out_width * depth <= 36 * 1024 * 1024
+    )
+    if fits:
+        return fused_shards((groups, rows, cols), amplitudes, factors, cycle_weight, orbital_order)
+    return plain_shards(amplitudes, factors, cycle_weight, orbital_order)
+
+
 def solution(mesh):
     return jax.shard_map(
         shards,

time: 220 us -> 110 us (0.50)
  waiting for transfers between devices: 130 us -> 0 us
  Pallas kernels: 0 us -> 103 us
  blocking collectives: 33.8 us -> 0 us
  matrix products: 28.2 us -> 0 us
  between operations: 14.1 us -> 0.64 us
  other arithmetic: 4.97 us -> 0 us
    pallas_call x0 -> x1, Pallas kernels: none -> 103 us  [fused_shards(): pl.pallas_call(functools.partial(kernel, sizes), out_shape=(jax.ShapeDtyp...]
    all_gather x1 -> x0, waiting for transfers between devices: 77.8 us -> none  [shards(): lax.all_gather(column_tile, 'col', axis=1, tiled=True)]
    reduce_scatter x1 -> x0, waiting for transfers between devices: 52.2 us -> none  [shards(): lax.psum_scatter(products, 'row', scatter_dimension=0, tiled=True)]
    dot_general x2 -> x0, matrix products: 28.2 us -> none  [the longest x1 24.1 us: shards(): lax.dot_general(lax.all_gather(column_tile, 'col', axis=1, tiled=True), c...]
    all_to_all x1 -> x0, blocking collectives: 18.1 us -> none  [shards(): lax.all_to_all(outgoing, ('grp', 'row'), split_axis=0, concat_axis=2, til...]
    all_gather x1 -> x0, blocking collectives: 15.7 us -> none  [shards(): lax.all_gather(factors, 'col', axis=0, tiled=True)]
    convert_element_type x1 -> x0, other arithmetic: 2.69 us -> none  [shards(): lax.psum_scatter(products, 'row', scatter_dimension=0, tiled=True)]
    unnamed x5 -> x2, local copies, waits for them, and re-layouts: 2.74 us -> 4.55 us
  transfers between devices with their start and end apart: 2 -> 0, of which waited for: 2 -> 0; matrix products, arithmetic and copies ran while one was open for 2% -> 0% of each run, Pallas kernels for 0% -> 0%
where the time goes in v1:
time: 110 us; the launch traced here: 108 us
  Pallas kernels  103 us (94%)
  local copies, waits for them, and re-layouts  4.55 us (4%)
    pallas_call x1, Pallas kernels, fused_shards(): pl.pallas_call(functools.partial(kernel, sizes), out_shape=(jax.ShapeDtyp...  103 us
    unnamed x2, local copies, waits for them, and re-layouts  4.55 us

profile of v1, /device:TPU:24, one launch (start us, length us, event | category | flops | bytes accessed | tf_op | source)
XLA Modules:
  0.0 108.1 jit_solution(17118598656293318515)
XLA Ops:
  0.6 103.0 %shard_map.59 = (bf16[8,256,256]{2,1,0:T(8,128)(2,1)}, bf16[128,4096]{1,0:T(8,128)(2,1)}) custom-call(s32[1,256]{1,0:T(1,128)} %bitcast.7, bf16[8,256,256]{2,1,0:T(8,128)(2,1)} %bitcast.6, bf16[1,256,256]{2,1,0:T(8,128)(2,1)} %fac.1, bf16[4096,4096]{1,0:T(8,128)(2,1)} %weight.1), custom_call_target="tpu_custom_call" | custom-call | flops 17179869184 | bytes 33554432 | tf_op jit(solution)/shard_map/pallas_call | solution.py:416
  103.6 2.3 %copy.9 = bf16[8,1,256,256]{3,2,1,0:T(8,128)(2,1)} copy(bf16[8,1,256,256]{3,2,1,0:T(8,128)(2,1)} %bitcast.5) | data formatting | bytes 2097152
  105.9 2.3 %copy.10 = bf16[128,4096]{1,0:T(8,128)(2,1)} copy(bf16[128,4096]{1,0:T(8,128)(2,1)} %get-tuple-element.11) | data formatting | bytes 2097152

commit v2 on v1

--- a/solution.py
+++ b/solution.py
@@ -109,15 +109,16 @@
         )
     pl.semaphore_wait(barrier, peers + cols - 1)
 
-    def raw_copy(s):
-        first = pl.multiple_of((s * 2 + 1 - core) * block, block)
+    def raw_copy(c, s):
+        first = pl.multiple_of((s * 2 + 1 - core) * block + c * TILE, TILE)
         return remote(
-            amp.at[:, pl.ds(first, block)], other.at[s], raw_send.at[s], raw_recv.at[s],
+            amp.at[:, pl.ds(first, TILE)], other.at[c, s], raw_send.at[c, s], raw_recv.at[c, s],
             at(g, mate, z),
         )
 
-    for s in range(sides):
-        raw_copy(s).start()
+    for c in range(chunks):
+        for s in range(sides):
+            raw_copy(c, s).start()
 
     load_fit.wait()
 
@@ -154,16 +155,45 @@
             ex_send.at[c, s * groups + q], ex_recv.at[c, chip], at(q, s * 2 + core, z),
         )
 
-    for s in range(sides):
-        raw_copy(s).wait_recv()
+    end_plane = (z == 0) | (z == cols - 1)
+    late_block = jnp.where(z == 0, 1, cols - 2)
+    late_in = end_plane & (late_block // 2 == side)
+    late_up = (z == cols - 2) & ((cols - 2) // 2 == side)
+    late_down = (z == 1) & (1 // 2 == side)
+    half = chunks // 2
+
+    def up_copy(j, c):
+        piece = panel.at[j, c]
+        return remote(piece, piece, up_send.at[j, c], z_recv.at[j, c], at(g, r, z + 1))
+
+    def down_copy(j, c):
+        piece = panel.at[j, c]
+        return remote(piece, piece, down_send.at[j, c], z_recv.at[j, c], at(g, r, z - 1))
+
+    def send_own(c):
+        for q in range(chips):
+            @pl.when(q != chip)
+            def _():
+                landing = panel.at[z, c, :, pl.ds(q * TILE, TILE), :]
+                remote(
+                    landing, landing, ex_send.at[c, 0], ex_recv.at[c, q], at(g, mate, z)
+                ).wait_recv()
+
+        @pl.when((z + 1 < cols) & jnp.logical_not(late_up & (c >= half)))
+        def _():
+            up_copy(z, c).start()
+
+        @pl.when((z > 0) & jnp.logical_not(late_down & (c >= half)))
+        def _():
+            down_copy(z, c).start()
 
     def exchange(c, carry):
+        for s in range(sides):
+            raw_copy(c, s).wait_recv()
         for s in range(sides):
             first = pl.multiple_of((s * 2 + core) * block + c * TILE, TILE)
             near = own[:, pl.ds(first, TILE), :].reshape(pairs * TILE, virtual)
-            far = other[s, :, pl.ds(pl.multiple_of(c * TILE, TILE), TILE), :].reshape(
-                pairs * TILE, virtual
-            )
+            far = other[c, s].reshape(pairs * TILE, virtual)
             both = jnp.concatenate([near, far], axis=0)
             picked = jnp.dot(both, pick, preferred_element_type=jnp.float32).astype(jnp.bfloat16)
             turned = jnp.dot(turn, picked, preferred_element_type=jnp.float32).astype(jnp.bfloat16)
@@ -180,34 +210,36 @@
                 def _():
                     staged[c, s, q] = part
                     ex_copy(c, s, q).start()
+
+        @pl.when(c > 0)
+        def _():
+            send_own(c - 1)
+
         return carry
 
     lax.fori_loop(0, chunks, exchange, 0)
-
-    def up_copy(j, c):
-        piece = panel.at[j, c]
-        return remote(piece, piece, up_send.at[j, c], z_recv.at[j, c], at(g, r, z + 1))
-
-    def down_copy(j, c):
-        piece = panel.at[j, c]
-        return remote(piece, piece, down_send.at[j, c], z_recv.at[j, c], at(g, r, z - 1))
-
-    def multiply(j, c, first):
+    send_own(chunks - 1)
+
+    def multiply(j, c):
         piece = panel[j, c].reshape(depth, panel_width)
 
         def one(i, carry):
             sl = pl.ds(pl.multiple_of(i * span, span), span)
             product = jnp.dot(wv[c, sl, :], piece, preferred_element_type=jnp.float32)
-            if first:
-                @pl.when(c == 0)
-                def _():
-                    acc[j, sl, :] = product
-
-                @pl.when(c > 0)
-                def _():
-                    acc[j, sl, :] += product
-            else:
-                acc[j, sl, :] = jnp.where(c == 0, product, acc[j, sl, :] + product)
+
+            @pl.when(c == 0)
+            def _():
+                acc[j, sl, :] = product
+
+            @pl.when(c > 0)
+            def _():
+                acc[j, sl, :] += product
+
+            @pl.when((c == chunks - 1) & (j % 2 != core))
+            def _():
+                pair_out[j // 2, sl, :] = acc[j, sl, :].astype(jnp.bfloat16)
+                pair_copy(j, i).start()
+
             return carry
 
         lax.fori_loop(0, PARTS, one, 0)
@@ -226,17 +258,6 @@
             far_out.at[sl], far_in.at[sl], far_send.at[i], far_recv.at[i],
             at(g, (1 - side) * 2 + core, z),
         )
-
-    def give(j):
-        @pl.when(j % 2 != core)
-        def _():
-            def one(i, carry):
-                sl = pl.ds(pl.multiple_of(i * span, span), span)
-                pair_out[j // 2, sl, :] = acc[j, sl, :].astype(jnp.bfloat16)
-                pair_copy(j, i).start()
-                return carry
-
-            lax.fori_loop(0, PARTS, one, 0)
 
     def pass_on(j):
         @pl.when((j % 2 == core) & (j // 2 != side))
@@ -251,29 +272,6 @@
 
             lax.fori_loop(0, PARTS, one, 0)
 
-    def first_hop(c, carry):
-        for q in range(chips):
-            @pl.when(q != chip)
-            def _():
-                landing = panel.at[z, c, :, pl.ds(q * TILE, TILE), :]
-                remote(
-                    landing, landing, ex_send.at[c, 0], ex_recv.at[c, q], at(g, mate, z)
-                ).wait_recv()
-
-        @pl.when(z + 1 < cols)
-        def _():
-            up_copy(z, c).start()
-
-        @pl.when(z > 0)
-        def _():
-            down_copy(z, c).start()
-
-        load_weight(c).wait()
-        multiply(z, c, True)
-        return carry
-
-    lax.fori_loop(0, chunks, first_hop, 0)
-
     def fan_copy(step):
         q = lax.rem(place + step, groups * rows)
         here = fitted.at[:, mine]
@@ -285,8 +283,6 @@
         fit_copy(step).wait_recv()
     for step in range(1, peers + 1):
         fan_copy(step).start()
-    give(z)
-    pass_on(z)
 
     def ladder(k):
         left = own[k]
@@ -298,11 +294,17 @@
             )
         own[k] = total.astype(jnp.bfloat16)
 
+    own_hop = jnp.where(end_plane, 1, cols - 2)
+    per_step = pairs // chunks
+
     def hop(n, carry):
         low, high = z - n, z + n
 
         def step(c, inner):
-            @pl.when(low >= 0)
+            on_time = jnp.logical_not(late_in & (n == 1) & (c >= half))
+            has_low, has_high = (low >= 0) & on_time, (high < cols) & on_time
+
+            @pl.when(has_low)
             def _():
                 up_copy(low, c).wait_recv()
 
@@ -310,7 +312,7 @@
                 def _():
                     up_copy(low, c).start()
 
-            @pl.when(high < cols)
+            @pl.when(has_high)
             def _():
                 down_copy(high, c).wait_recv()
 
@@ -318,41 +320,72 @@
                 def _():
                     down_copy(high, c).start()
 
-            @pl.when(low >= 0)
-            def _():
-                multiply(low, c, True)
-
-            @pl.when(high < cols)
-            def _():
-                multiply(high, c, True)
+            @pl.when((n == cols - 2) & (c == chunks - 1))
+            def _():
+                @pl.when(late_up)
+                def _():
+                    for d in range(half, chunks):
+                        up_copy(z, d).start()
+
+                @pl.when(late_down)
+                def _():
+                    for d in range(half, chunks):
+                        down_copy(z, d).start()
+
+            @pl.when(n == 1)
+            def _():
+                load_weight(c).wait()
+
+            @pl.when(has_low)
+            def _():
+                multiply(low, c)
+
+            @pl.when(has_high)
+            def _():
+                multiply(high, c)
+
+            @pl.when(n == own_hop)
+            def _():
+                multiply(z, c)
+
+            @pl.when(n == own_hop + 1)
+            def _():
+                @pl.when(c == 0)
+                def _():
+                    for step in range(1, peers + 1):
+                        fan_copy(step).wait_recv()
+
+                for k in range(per_step):
+                    ladder(c * per_step + k)
 
             return inner
 
         lax.fori_loop(0, chunks, step, 0)
-        for j, valid in ((low, low >= 0), (high, high < cols)):
+        whole = jnp.logical_not(late_in & (n == 1))
+        for j, valid in ((low, (low >= 0) & whole), (high, (high < cols) & whole), (z, n == own_hop)):
             @pl.when(valid)
             def _():
-                give(j)
-        for j, valid in ((low, low >= 0), (high, high < cols)):
-            @pl.when(valid)
-            def _():
                 pass_on(j)
 
-        @pl.when(n == 1)
+        @pl.when(n == own_hop + 1)
         def _():
-            for step in range(1, peers + 1):
-                fan_copy(step).wait_recv()
-
-            def one(k, inner):
-                ladder(k)
-                return inner
-
-            lax.fori_loop(0, pairs, one, 0)
             pltpu.make_async_copy(own, ladder_out, load_sem.at[0]).start()
 
         return carry
 
     lax.fori_loop(1, cols, hop, 0)
+
+    @pl.when(late_in)
+    def _():
+        def step(c, carry):
+            piece = panel.at[late_block, c]
+            remote(
+                piece, piece, up_send.at[late_block, c], z_recv.at[late_block, c], at(g, mate, z)
+            ).wait_recv()
+            multiply(late_block, c)
+            return carry
+
+        lax.fori_loop(half, chunks, step, 0)
 
     def out_copy(i):
         return pltpu.make_async_copy(
@@ -369,8 +402,6 @@
         out_copy(i).start()
 
     pltpu.make_async_copy(own, ladder_out, load_sem.at[0]).wait()
-    for s in range(sides):
-        raw_copy(s).wait_send()
     for step in range(1, cols):
         fit_copy(step).wait_send()
     for step in range(1, peers + 1):
@@ -378,6 +409,7 @@
 
     def drain(c, carry):
         for s in range(sides):
+            raw_copy(c, s).wait_send()
             for q in range(groups):
                 @pl.when(jnp.logical_not((q == g) & (s == side)))
                 def _():
@@ -398,6 +430,19 @@
             pair_copy(2 * h, i).wait_send()
         far_copy(i).wait_send()
         out_copy(i).wait()
+
+
+def hand_over(ladder_in, cycle_in, ladder_out, cycle_out, sem):
+    moves = []
+    for n, (source, target) in enumerate(((ladder_in, ladder_out), (cycle_in, cycle_out))):
+        size = source.shape[0] // PARTS
+        for i in range(PARTS):
+            sl = pl.ds(i * size, size)
+            moves.append(pltpu.make_async_copy(source.at[sl], target.at[sl], sem.at[n, i]))
+    for move in moves:
+        move.start()
+    for move in moves:
+        move.wait()
 
 
 def fused_shards(sizes, amplitudes, factors, cycle_weight, orbital_order):
@@ -424,7 +469,7 @@
         scratch_shapes=[
             pltpu.VMEM((chunks, out_width, depth // chunks), half),
             pltpu.VMEM((pairs, virtual, virtual), half),
-            pltpu.VMEM((rows // 2, pairs, block, virtual), half),
+            pltpu.VMEM((chunks, rows // 2, pairs, TILE, virtual), half),
             pltpu.VMEM((chunks, rows // 2, groups, TILE, 2 * pairs, panel_width), half),
             pltpu.VMEM((cols, chunks, TILE, 2 * pairs * chips, panel_width), half),
             pltpu.VMEM((cols, out_width, panel_width), jnp.float32),
@@ -436,8 +481,8 @@
             pltpu.VMEM((cols, virtual, virtual), half),
             dma((2,)),
             dma((chunks,)),
-            dma((rows // 2,)),
-            dma((rows // 2,)),
+            dma((chunks, rows // 2)),
+            dma((chunks, rows // 2)),
             dma((chunks, chips)),
             dma((chunks, chips)),
             dma((cols, chunks)),
@@ -465,6 +510,17 @@
         factors,
         cycle_weight,
     )
+    ladder_term, cycle_term = pl.pallas_call(
+        hand_over,
+        out_shape=(
+            jax.ShapeDtypeStruct(ladder_term.shape, half),
+            jax.ShapeDtypeStruct(cycle_term.shape, half),
+        ),
+        in_specs=[anywhere, anywhere],
+        out_specs=(anywhere, anywhere),
+        scratch_shapes=[dma((2, PARTS))],
+        compiler_params=pltpu.CompilerParams(vmem_limit_bytes=60 * 1024 * 1024),
+    )(ladder_term, cycle_term)
     return ladder_term.reshape(pairs, one, virtual, virtual), cycle_term
 
 
@@ -481,6 +537,8 @@
         and 2 * pairs == TILE
         and virtual == groups * LANES
         and virtual % (rows * TILE) == 0
+        and pairs % (virtual // (rows * TILE)) == 0
+        and virtual // (rows * TILE) > 1
         and virtual % (groups * rows * TILE) == 0
         and depth == virtual // rows * groups * rows * pairs
         and out_width % (PARTS * LANES) == 0

time: 110 us -> 161 us (1.46); the launches traced: 108 us -> 161 us
  Pallas kernels: 103 us -> 160 us
  local copies, waits for them, and re-layouts: 4.55 us -> 0 us
    pallas_call x0 -> x1, Pallas kernels: none -> 64.7 us  [fused_shards(): pl.pallas_call(hand_over, out_shape=(jax.ShapeDtypeStruct(ladder_term.sha...]
    pallas_call x1, Pallas kernels: 103 us -> 95.5 us  [fused_shards(): pl.pallas_call(functools.partial(kernel, sizes), out_shape=(jax.ShapeDtyp...]
    unnamed x2 -> x0, local copies, waits for them, and re-layouts: 4.55 us -> none
where the time goes in v2:
time: 161 us
  Pallas kernels  160 us (99%)
    pallas_call x1, Pallas kernels, fused_shards(): pl.pallas_call(functools.partial(kernel, sizes), out_shape=(jax.ShapeDtyp...  95.5 us
    pallas_call x1, Pallas kernels, fused_shards(): pl.pallas_call(hand_over, out_shape=(jax.ShapeDtypeStruct(ladder_term.sha...  64.7 us

profile of v2, /device:TPU:24, one launch (start us, length us, event | category | flops | bytes accessed | tf_op | source)
XLA Modules:
  0.0 160.9 jit_solution(18069532301878620479)
XLA Ops:
  0.6 95.5 %shard_map.59 = (bf16[8,256,256]{2,1,0:T(8,128)(2,1)}, bf16[128,4096]{1,0:T(8,128)(2,1)}) custom-call(s32[1,256]{1,0:T(1,128)} %bitcast.7, bf16[8,256,256]{2,1,0:T(8,128)(2,1)} %bitcast.5, bf16[1,256,256]{2,1,0:T(8,128)(2,1)} %fac.1, bf16[4096,4096]{1,0:T(8,128)(2,1)} %weight.1), custom_call_target="tpu_custom_call" | custom-call | flops 17179869184 | bytes 33554432 | tf_op jit(solution)/shard_map/pallas_call | solution.py:461
  96.2 64.7 %shard_map.60 = (bf16[8,256,256]{2,1,0:T(8,128)(2,1)}, bf16[128,4096]{1,0:T(8,128)(2,1)}) custom-call(bf16[8,256,256]{2,1,0:T(8,128)(2,1)} %get-tuple-element.6.ladder_in, bf16[128,4096]{1,0:T(8,128)(2,1)} %get-tuple-element.7.cycle_in), custom_call_target="tpu_custom_call" | custom-call | tf_op jit(solution)/shard_map/pallas_call | solution.py:513

commit v3 on v2

--- a/solution.py
+++ b/solution.py
@@ -220,25 +220,27 @@
     lax.fori_loop(0, chunks, exchange, 0)
     send_own(chunks - 1)
 
-    def multiply(j, c):
-        piece = panel[j, c].reshape(depth, panel_width)
+    def multiply(blocks, c):
+        piece = jnp.concatenate([panel[j, c].reshape(depth, panel_width) for j in blocks], axis=1)
 
         def one(i, carry):
             sl = pl.ds(pl.multiple_of(i * span, span), span)
             product = jnp.dot(wv[c, sl, :], piece, preferred_element_type=jnp.float32)
-
-            @pl.when(c == 0)
-            def _():
-                acc[j, sl, :] = product
-
-            @pl.when(c > 0)
-            def _():
-                acc[j, sl, :] += product
-
-            @pl.when((c == chunks - 1) & (j % 2 != core))
-            def _():
-                pair_out[j // 2, sl, :] = acc[j, sl, :].astype(jnp.bfloat16)
-                pair_copy(j, i).start()
+            for n, j in enumerate(blocks):
+                part = product[:, n * panel_width:(n + 1) * panel_width]
+
+                @pl.when(c == 0)
+                def _():
+                    acc[j, sl, :] = part
+
+                @pl.when(c > 0)
+                def _():
+                    acc[j, sl, :] += part
+
+                @pl.when((c == chunks - 1) & (j % 2 != core))
+                def _():
+                    pair_out[j // 2, sl, :] = acc[j, sl, :].astype(jnp.bfloat16)
+                    pair_copy(j, i).start()
 
             return carry
 
@@ -336,17 +338,16 @@
             def _():
                 load_weight(c).wait()
 
-            @pl.when(has_low)
-            def _():
-                multiply(low, c)
-
-            @pl.when(has_high)
-            def _():
-                multiply(high, c)
-
-            @pl.when(n == own_hop)
-            def _():
-                multiply(z, c)
+            inside = (n == 1) & jnp.logical_not(end_plane)
+            other = jnp.where(low >= 0, low, high)
+
+            @pl.when(inside | ((n == own_hop) & on_time))
+            def _():
+                multiply((jnp.where(inside, low, z), jnp.where(inside, high, other)), c)
+
+            @pl.when(end_plane & ((n > 1) | jnp.logical_not(on_time)))
+            def _():
+                multiply((jnp.where(n > 1, other, z),), c)
 
             @pl.when(n == own_hop + 1)
             def _():
@@ -382,7 +383,7 @@
             remote(
                 piece, piece, up_send.at[late_block, c], z_recv.at[late_block, c], at(g, mate, z)
             ).wait_recv()
-            multiply(late_block, c)
+            multiply((late_block,), c)
             return carry
 
         lax.fori_loop(half, chunks, step, 0)
@@ -398,7 +399,7 @@
         far_copy(i).wait_recv()
         total = acc[r, sl, :] + pair_in[side, sl, :].astype(jnp.float32)
         total += far_in[sl, :].astype(jnp.float32)
-        result[i] = total.T.astype(jnp.bfloat16)
+        result[i] = total.astype(jnp.bfloat16).T
         out_copy(i).start()
 
     pltpu.make_async_copy(own, ladder_out, load_sem.at[0]).wait()
@@ -432,17 +433,22 @@
         out_copy(i).wait()
 
 
-def hand_over(ladder_in, cycle_in, ladder_out, cycle_out, sem):
-    moves = []
-    for n, (source, target) in enumerate(((ladder_in, ladder_out), (cycle_in, cycle_out))):
+def hand_over(ladder_in, cycle_in, ladder_out, cycle_out, ladder_held, cycle_held, sem):
+    fetches, stores = [], []
+    whole = ((ladder_in, ladder_held, ladder_out), (cycle_in, cycle_held, cycle_out))
+    for n, (source, held, target) in enumerate(whole):
         size = source.shape[0] // PARTS
         for i in range(PARTS):
             sl = pl.ds(i * size, size)
-            moves.append(pltpu.make_async_copy(source.at[sl], target.at[sl], sem.at[n, i]))
-    for move in moves:
-        move.start()
-    for move in moves:
-        move.wait()
+            fetches.append(pltpu.make_async_copy(source.at[sl], held.at[sl], sem.at[0, n, i]))
+            stores.append(pltpu.make_async_copy(held.at[sl], target.at[sl], sem.at[1, n, i]))
+    for fetch in fetches:
+        fetch.start()
+    for fetch, store in zip(fetches, stores):
+        fetch.wait()
+        store.start()
+    for store in stores:
+        store.wait()
 
 
 def fused_shards(sizes, amplitudes, factors, cycle_weight, orbital_order):
@@ -518,7 +524,11 @@
         ),
         in_specs=[anywhere, anywhere],
         out_specs=(anywhere, anywhere),
-        scratch_shapes=[dma((2, PARTS))],
+        scratch_shapes=[
+            pltpu.VMEM(ladder_term.shape, half),
+            pltpu.VMEM(cycle_term.shape, half),
+            dma((2, 2, PARTS)),
+        ],
         compiler_params=pltpu.CompilerParams(vmem_limit_bytes=60 * 1024 * 1024),
     )(ladder_term, cycle_term)
     return ladder_term.reshape(pairs, one, virtual, virtual), cycle_term

time: 161 us -> 96.3 us (0.60)
  Pallas kernels: 160 us -> 95.5 us
    pallas_call x1, Pallas kernels: 64.7 us -> 2.4 us  [fused_shards(): pl.pallas_call(hand_over, out_shape=(jax.ShapeDtypeStruct(ladder_term.sha...]
    pallas_call x1, Pallas kernels: 95.5 us -> 93.1 us  [fused_shards(): pl.pallas_call(functools.partial(kernel, sizes), out_shape=(jax.ShapeDtyp...]
where the time goes in v3:
time: 96.3 us; the launch traced here: 96.2 us
  Pallas kernels  95.5 us (99%)
    pallas_call x1, Pallas kernels, fused_shards(): pl.pallas_call(functools.partial(kernel, sizes), out_shape=(jax.ShapeDtyp...  93.1 us
    pallas_call x1, Pallas kernels, fused_shards(): pl.pallas_call(hand_over, out_shape=(jax.ShapeDtypeStruct(ladder_term.sha...  2.4 us

profile of v3, /device:TPU:24, one launch (start us, length us, event | category | flops | bytes accessed | tf_op | source)
XLA Modules:
  0.0 96.2 jit_solution(14032682795695249352)
XLA Ops:
  0.6 93.1 %shard_map.59 = (bf16[8,256,256]{2,1,0:T(8,128)(2,1)}, bf16[128,4096]{1,0:T(8,128)(2,1)}) custom-call(s32[1,256]{1,0:T(1,128)} %bitcast.7, bf16[8,256,256]{2,1,0:T(8,128)(2,1)} %bitcast.5, bf16[1,256,256]{2,1,0:T(8,128)(2,1)} %fac.1, bf16[4096,4096]{1,0:T(8,128)(2,1)} %weight.1), custom_call_target="tpu_custom_call" | custom-call | flops 17179869184 | bytes 33554432 | tf_op jit(solution)/shard_map/pallas_call | solution.py:467
  93.8 2.4 %shard_map.60 = (bf16[8,256,256]{2,1,0:T(8,128)(2,1)}, bf16[128,4096]{1,0:T(8,128)(2,1)}) custom-call(bf16[8,256,256]{2,1,0:T(8,128)(2,1)} %get-tuple-element.6.ladder_in, bf16[128,4096]{1,0:T(8,128)(2,1)} %get-tuple-element.7.cycle_in), custom_call_target="tpu_custom_call" | custom-call | tf_op jit(solution)/shard_map/pallas_call | solution.py:519

commit v4 on v3

--- a/solution.py
+++ b/solution.py
@@ -162,30 +162,63 @@
     late_down = (z == 1) & (1 // 2 == side)
     half = chunks // 2
 
-    def up_copy(j, c):
-        piece = panel.at[j, c]
-        return remote(piece, piece, up_send.at[j, c], z_recv.at[j, c], at(g, r, z + 1))
-
-    def down_copy(j, c):
-        piece = panel.at[j, c]
-        return remote(piece, piece, down_send.at[j, c], z_recv.at[j, c], at(g, r, z - 1))
+    fine = TILE // chips
+
+    def piece_of(j, c, f, striped):
+        if striped:
+            return panel.at[j, c, :, pl.ds(pl.multiple_of(f * TILE, TILE), TILE), :]
+        return panel.at[j, c, pl.ds(f * fine, fine)]
+
+    def up_copy(j, c, f, striped):
+        piece = piece_of(j, c, f, striped)
+        return remote(piece, piece, up_send.at[j, c, f], z_recv.at[j, c, f], at(g, r, z + 1))
+
+    def down_copy(j, c, f, striped):
+        piece = piece_of(j, c, f, striped)
+        return remote(piece, piece, down_send.at[j, c, f], z_recv.at[j, c, f], at(g, r, z - 1))
+
+    def for_pieces(c, act):
+        @pl.when(c == 0)
+        def _():
+            for i in range(chips):
+                act(lax.rem(chip + i, chips), True)
+
+        @pl.when(c > 0)
+        def _():
+            for f in range(chips):
+                act(f, False)
+
+    def arrived(c, q):
+        @pl.when(q != chip)
+        def _():
+            landing = piece_of(z, c, q, True)
+            remote(
+                landing, landing, ex_send.at[c, 0], ex_recv.at[c, q], at(g, mate, z)
+            ).wait_recv()
+
+    def send_piece(c, f, striped):
+        @pl.when((z + 1 < cols) & jnp.logical_not(late_up & (c >= half)))
+        def _():
+            up_copy(z, c, f, striped).start()
+
+        @pl.when((z > 0) & jnp.logical_not(late_down & (c >= half)))
+        def _():
+            down_copy(z, c, f, striped).start()
 
     def send_own(c):
-        for q in range(chips):
-            @pl.when(q != chip)
-            def _():
-                landing = panel.at[z, c, :, pl.ds(q * TILE, TILE), :]
-                remote(
-                    landing, landing, ex_send.at[c, 0], ex_recv.at[c, q], at(g, mate, z)
-                ).wait_recv()
-
-        @pl.when((z + 1 < cols) & jnp.logical_not(late_up & (c >= half)))
-        def _():
-            up_copy(z, c).start()
-
-        @pl.when((z > 0) & jnp.logical_not(late_down & (c >= half)))
-        def _():
-            down_copy(z, c).start()
+        @pl.when(c == 0)
+        def _():
+            for i in range(1, chips):
+                q = lax.rem(chip + i, chips)
+                arrived(0, q)
+                send_piece(0, q, True)
+
+        @pl.when(c > 0)
+        def _():
+            for q in range(chips):
+                arrived(c, q)
+            for f in range(chips):
+                send_piece(c, f, False)
 
     def exchange(c, carry):
         for s in range(sides):
@@ -211,6 +244,10 @@
                     staged[c, s, q] = part
                     ex_copy(c, s, q).start()
 
+        @pl.when(c == 0)
+        def _():
+            send_piece(0, chip, True)
+
         @pl.when(c > 0)
         def _():
             send_own(c - 1)
@@ -218,14 +255,23 @@
         return carry
 
     lax.fori_loop(0, chunks, exchange, 0)
-    send_own(chunks - 1)
-
-    def multiply(blocks, c):
-        piece = jnp.concatenate([panel[j, c].reshape(depth, panel_width) for j in blocks], axis=1)
+    send_own(jnp.int32(chunks - 1))
+
+    def multiply(blocks, c, f=None):
+        if f is None:
+            wide, start, last = depth, 0, True
+            held = [panel[j, c].reshape(depth, panel_width) for j in blocks]
+        else:
+            wide, last = depth // chips, f == chips - 1
+            start = pl.multiple_of(f * wide, wide)
+            held = [panel[j, c, pl.ds(f * fine, fine)].reshape(wide, panel_width) for j in blocks]
+        piece = jnp.concatenate(held, axis=1)
 
         def one(i, carry):
             sl = pl.ds(pl.multiple_of(i * span, span), span)
-            product = jnp.dot(wv[c, sl, :], piece, preferred_element_type=jnp.float32)
+            product = jnp.dot(
+                wv[c, sl, pl.ds(start, wide)], piece, preferred_element_type=jnp.float32
+            )
             for n, j in enumerate(blocks):
                 part = product[:, n * panel_width:(n + 1) * panel_width]
 
@@ -237,7 +283,7 @@
                 def _():
                     acc[j, sl, :] += part
 
-                @pl.when((c == chunks - 1) & (j % 2 != core))
+                @pl.when((c == chunks - 1) & last & (j % 2 != core))
                 def _():
                     pair_out[j // 2, sl, :] = acc[j, sl, :].astype(jnp.bfloat16)
                     pair_copy(j, i).start()
@@ -299,6 +345,20 @@
     own_hop = jnp.where(end_plane, 1, cols - 2)
     per_step = pairs // chunks
 
+    def await_piece(j, c, f):
+        piece = piece_of(j, c, f, False)
+        remote(piece, piece, up_send.at[j, c, f], z_recv.at[j, c, f], at(g, mate, z)).wait_recv()
+
+    def finish(j):
+        c = jnp.int32(chunks - 1)
+
+        def one(f, carry):
+            await_piece(j, c, f)
+            multiply((j,), c, f)
+            return carry
+
+        lax.fori_loop(0, chips, one, 0)
+
     def hop(n, carry):
         low, high = z - n, z + n
 
@@ -306,33 +366,38 @@
             on_time = jnp.logical_not(late_in & (n == 1) & (c >= half))
             has_low, has_high = (low >= 0) & on_time, (high < cols) & on_time
 
-            @pl.when(has_low)
-            def _():
-                up_copy(low, c).wait_recv()
-
-                @pl.when(z + 1 < cols)
-                def _():
-                    up_copy(low, c).start()
-
-            @pl.when(has_high)
-            def _():
-                down_copy(high, c).wait_recv()
-
-                @pl.when(z > 0)
-                def _():
-                    down_copy(high, c).start()
+            ending = end_plane & (n == cols - 1) & (c == chunks - 1) & jnp.logical_not(late_in)
+
+            @pl.when(has_low & jnp.logical_not(ending))
+            def _():
+                def act(f, striped):
+                    up_copy(low, c, f, striped).wait_recv()
+
+                    @pl.when(z + 1 < cols)
+                    def _():
+                        up_copy(low, c, f, striped).start()
+
+                for_pieces(c, act)
+
+            @pl.when(has_high & jnp.logical_not(ending))
+            def _():
+                def act(f, striped):
+                    down_copy(high, c, f, striped).wait_recv()
+
+                    @pl.when(z > 0)
+                    def _():
+                        down_copy(high, c, f, striped).start()
+
+                for_pieces(c, act)
 
             @pl.when((n == cols - 2) & (c == chunks - 1))
             def _():
-                @pl.when(late_up)
-                def _():
-                    for d in range(half, chunks):
-                        up_copy(z, d).start()
-
-                @pl.when(late_down)
-                def _():
-                    for d in range(half, chunks):
-                        down_copy(z, d).start()
+                for late, copy in ((late_up, up_copy), (late_down, down_copy)):
+                    @pl.when(late)
+                    def _():
+                        for d in range(half, chunks):
+                            for f in range(chips):
+                                copy(z, d, f, False).start()
 
             @pl.when(n == 1)
             def _():
@@ -345,9 +410,13 @@
             def _():
                 multiply((jnp.where(inside, low, z), jnp.where(inside, high, other)), c)
 
-            @pl.when(end_plane & ((n > 1) | jnp.logical_not(on_time)))
+            @pl.when(end_plane & ((n > 1) | jnp.logical_not(on_time)) & jnp.logical_not(ending))
             def _():
                 multiply((jnp.where(n > 1, other, z),), c)
+
+            @pl.when(ending)
+            def _():
+                finish(other)
 
             @pl.when(n == own_hop + 1)
             def _():
@@ -379,14 +448,13 @@
     @pl.when(late_in)
     def _():
         def step(c, carry):
-            piece = panel.at[late_block, c]
-            remote(
-                piece, piece, up_send.at[late_block, c], z_recv.at[late_block, c], at(g, mate, z)
-            ).wait_recv()
+            for f in range(chips):
+                await_piece(late_block, c, f)
             multiply((late_block,), c)
             return carry
 
-        lax.fori_loop(half, chunks, step, 0)
+        lax.fori_loop(half, chunks - 1, step, 0)
+        finish(late_block)
 
     def out_copy(i):
         return pltpu.make_async_copy(
@@ -418,11 +486,11 @@
         for j in range(cols):
             @pl.when((j <= z) & (z + 1 < cols))
             def _():
-                up_copy(j, c).wait_send()
+                for_pieces(c, lambda f, striped: up_copy(j, c, f, striped).wait_send())
 
             @pl.when((j >= z) & (z > 0))
             def _():
-                down_copy(j, c).wait_send()
+                for_pieces(c, lambda f, striped: down_copy(j, c, f, striped).wait_send())
         return carry
 
     lax.fori_loop(0, chunks, drain, 0)
@@ -491,9 +559,9 @@
             dma((chunks, rows // 2)),
             dma((chunks, chips)),
             dma((chunks, chips)),
-            dma((cols, chunks)),
-            dma((cols, chunks)),
-            dma((cols, chunks)),
+            dma((cols, chunks, chips)),
+            dma((cols, chunks, chips)),
+            dma((cols, chunks, chips)),
             dma((cols - 1,)),
             dma((cols - 1,)),
             dma((groups * rows - 1,)),
@@ -545,6 +613,7 @@
         and rows // 2 == 2
         and rows % 2 == 0
         and 2 * pairs == TILE
+        and TILE % (groups * rows // 2) == 0
         and virtual == groups * LANES
         and virtual % (rows * TILE) == 0
         and pairs % (virtual // (rows * TILE)) == 0

time: 96.3 us -> 95.5 us (level)
  Pallas kernels: 95.5 us -> 94.4 us
    pallas_call x1, Pallas kernels: 93.1 us -> 92 us  [fused_shards(): pl.pallas_call(functools.partial(kernel, sizes), out_shape=(jax.ShapeDtyp...]
where the time goes in v4:
time: 95.5 us; the launch traced here: 95.1 us
  Pallas kernels  94.4 us (99%)
    pallas_call x1, Pallas kernels, fused_shards(): pl.pallas_call(functools.partial(kernel, sizes), out_shape=(jax.ShapeDtyp...  92 us
    pallas_call x1, Pallas kernels, fused_shards(): pl.pallas_call(hand_over, out_shape=(jax.ShapeDtypeStruct(ladder_term.sha...  2.4 us

profile of v4, /device:TPU:24, one launch (start us, length us, event | category | flops | bytes accessed | tf_op | source)
XLA Modules:
  0.0 95.1 jit_solution(16965955458640235135)
XLA Ops:
  0.6 92.0 %shard_map.59 = (bf16[8,256,256]{2,1,0:T(8,128)(2,1)}, bf16[128,4096]{1,0:T(8,128)(2,1)}) custom-call(s32[1,256]{1,0:T(1,128)} %bitcast.7, bf16[8,256,256]{2,1,0:T(8,128)(2,1)} %bitcast.5, bf16[1,256,256]{2,1,0:T(8,128)(2,1)} %fac.1, bf16[4096,4096]{1,0:T(8,128)(2,1)} %weight.1), custom_call_target="tpu_custom_call" | custom-call | flops 17179869184 | bytes 33554432 | tf_op jit(solution)/shard_map/pallas_call | solution.py:535
  92.7 2.4 %shard_map.60 = (bf16[8,256,256]{2,1,0:T(8,128)(2,1)}, bf16[128,4096]{1,0:T(8,128)(2,1)}) custom-call(bf16[8,256,256]{2,1,0:T(8,128)(2,1)} %get-tuple-element.6.ladder_in, bf16[128,4096]{1,0:T(8,128)(2,1)} %get-tuple-element.7.cycle_in), custom_call_target="tpu_custom_call" | custom-call | tf_op jit(solution)/shard_map/pallas_call | solution.py:587

commit v5 on v4

--- a/solution.py
+++ b/solution.py
@@ -342,19 +342,22 @@
             )
         own[k] = total.astype(jnp.bfloat16)
 
-    own_hop = jnp.where(end_plane, 1, cols - 2)
+    natural = end_plane & jnp.logical_not(late_in)
+    before_last = jnp.where(z == 0, cols - 2, 1)
+    own_hop = jnp.where(natural, 1, cols - 2)
+    ladder_hop = jnp.where(late_in, 1, own_hop + 1)
     per_step = pairs // chunks
 
     def await_piece(j, c, f):
         piece = piece_of(j, c, f, False)
         remote(piece, piece, up_send.at[j, c, f], z_recv.at[j, c, f], at(g, mate, z)).wait_recv()
 
-    def finish(j):
+    def finish(blocks):
         c = jnp.int32(chunks - 1)
 
         def one(f, carry):
-            await_piece(j, c, f)
-            multiply((j,), c, f)
+            await_piece(blocks[-1], c, f)
+            multiply(blocks, c, f)
             return carry
 
         lax.fori_loop(0, chips, one, 0)
@@ -406,19 +409,26 @@
             inside = (n == 1) & jnp.logical_not(end_plane)
             other = jnp.where(low >= 0, low, high)
 
-            @pl.when(inside | ((n == own_hop) & on_time))
-            def _():
-                multiply((jnp.where(inside, low, z), jnp.where(inside, high, other)), c)
-
-            @pl.when(end_plane & ((n > 1) | jnp.logical_not(on_time)) & jnp.logical_not(ending))
-            def _():
-                multiply((jnp.where(n > 1, other, z),), c)
+            closing = end_plane & (n == cols - 1)
+            beside = jnp.where(late_in, late_block, before_last)
+            one_only = closing & late_in & (c >= half)
+            first = jnp.where(inside, low, jnp.where(closing, beside, z))
+
+            @pl.when(
+                inside | (n == own_hop) | (closing & jnp.logical_not(one_only | ending))
+            )
+            def _():
+                multiply((first, jnp.where(inside, high, other)), c)
+
+            @pl.when(one_only)
+            def _():
+                multiply((other,), c)
 
             @pl.when(ending)
             def _():
-                finish(other)
-
-            @pl.when(n == own_hop + 1)
+                finish((before_last, other))
+
+            @pl.when(n == ladder_hop)
             def _():
                 @pl.when(c == 0)
                 def _():
@@ -431,13 +441,22 @@
             return inner
 
         lax.fori_loop(0, chunks, step, 0)
-        whole = jnp.logical_not(late_in & (n == 1))
-        for j, valid in ((low, (low >= 0) & whole), (high, (high < cols) & whole), (z, n == own_hop)):
+        inside = (n == 1) & jnp.logical_not(end_plane)
+        closing = end_plane & (n == cols - 1)
+        other = jnp.where(low >= 0, low, high)
+        done = (
+            (low, inside),
+            (high, inside),
+            (z, n == own_hop),
+            (other, (n == own_hop) | closing),
+            (before_last, closing & natural),
+        )
+        for j, valid in done:
             @pl.when(valid)
             def _():
                 pass_on(j)
 
-        @pl.when(n == own_hop + 1)
+        @pl.when(n == ladder_hop)
         def _():
             pltpu.make_async_copy(own, ladder_out, load_sem.at[0]).start()
 
@@ -454,7 +473,7 @@
             return carry
 
         lax.fori_loop(half, chunks - 1, step, 0)
-        finish(late_block)
+        finish((late_block,))
 
     def out_copy(i):
         return pltpu.make_async_copy(

time: 95.5 us -> 95.9 us (level)
  no operation moved by 1% of the time
where the time goes in v5:
time: 95.9 us; the launch traced here: 95.1 us
  Pallas kernels  94.4 us (98%)
    pallas_call x1, Pallas kernels, fused_shards(): pl.pallas_call(functools.partial(kernel, sizes), out_shape=(jax.ShapeDtyp...  92 us
    pallas_call x1, Pallas kernels, fused_shards(): pl.pallas_call(hand_over, out_shape=(jax.ShapeDtypeStruct(ladder_term.sha...  2.4 us

profile of v5, /device:TPU:24, one launch (start us, length us, event | category | flops | bytes accessed | tf_op | source)
XLA Modules:
  0.0 95.1 jit_solution(9517273412426828822)
XLA Ops:
  0.6 92.0 %shard_map.59 = (bf16[8,256,256]{2,1,0:T(8,128)(2,1)}, bf16[128,4096]{1,0:T(8,128)(2,1)}) custom-call(s32[1,256]{1,0:T(1,128)} %bitcast.7, bf16[8,256,256]{2,1,0:T(8,128)(2,1)} %bitcast.5, bf16[1,256,256]{2,1,0:T(8,128)(2,1)} %fac.1, bf16[4096,4096]{1,0:T(8,128)(2,1)} %weight.1), custom_call_target="tpu_custom_call" | custom-call | flops 17179869184 | bytes 33554432 | tf_op jit(solution)/shard_map/pallas_call | solution.py:554
  92.7 2.4 %shard_map.60 = (bf16[8,256,256]{2,1,0:T(8,128)(2,1)}, bf16[128,4096]{1,0:T(8,128)(2,1)}) custom-call(bf16[8,256,256]{2,1,0:T(8,128)(2,1)} %get-tuple-element.6.ladder_in, bf16[128,4096]{1,0:T(8,128)(2,1)} %get-tuple-element.7.cycle_in), custom_call_target="tpu_custom_call" | custom-call | tf_op jit(solution)/shard_map/pallas_call | solution.py:606
